TPU v7x, 32 devices: a whole 2x2x4 slice. The times are simulated.
32 devices in a mesh: groups: 2 (over y), ep: 4 (over x, core), tp: 4 (over z).
Axes of the slice: x: 2, y: 2, z: 4, core: 2. Of those that a mesh axis runs over, the one named last changes fastest.
Arguments:
- hidden_in: bfloat16 [32, 4, 3584], P(('groups', 'ep', 'tp')), parts along dimension 0, may hold values from -12 to 12
- queries: bfloat16 [32, 4, 128, 576], P(('groups', 'ep', 'tp')), parts along dimension 0, may hold values from -100 to 100
- kv_cache: bfloat16 [32, 2048, 576], P(('groups', 'ep', 'tp')), parts along dimension 0, may hold values from -6 to 6
- new_kv: bfloat16 [32, 4, 576], P(('groups', 'ep', 'tp')), parts along dimension 0, may hold values from -8 to 8
- lengths: int32 [32], P(('groups', 'ep', 'tp')), parts along dimension 0, may hold values from 128 to 2048, as said below
- expert_ids: int32 [32, 4, 2], P(('groups', 'ep')), parts along dimension 0, may hold values from 0 to 3, all different within a row; in each aligned block of 16 rows (0 to 15, 16 to 31, ..., all dimensions but the last counted through in order) at most 12 rows name the same one
- value_up: bfloat16 [128, 512, 128], P(('ep', 'tp')), may hold values from -3 to 3
- out_proj: bfloat16 [128, 128, 3584], P(('ep', 'tp')), may hold values from -0.046875 to 0.046875
- norm_gain: bfloat16 [3584], replicated, may hold values from 0.099609375 to 1.8984375
- router: bfloat16 [3584, 4], replicated, may hold values from -0.09375 to 0.09375
- expert_in: bfloat16 [4, 2, 3584, 2048], P('ep', None, None, 'tp'), may hold values from -0.09375 to 0.09375
- expert_out: bfloat16 [4, 2048, 3584], P('ep', 'tp'), may hold values from -0.125 to 0.125
- shared_in: bfloat16 [2, 3584, 1024], P(None, None, 'tp'), may hold values from -0.09375 to 0.09375
- shared_out: bfloat16 [1024, 3584], P('tp'), may hold values from -0.1875 to 0.1875
Outputs:
- layer_out: bfloat16 [32, 4, 3584], P(('groups', 'ep', 'tp')), parts along dimension 0
There are 2 independent parts, one for each index of `groups`. A program takes and returns all parts, laid end to end along the dimension named above; an argument that names none is the same for every part. Nothing has to cross between parts.
Inputs may be any that keep to these rules, and one draw needn't show every extreme that they name: `expert_ids`: each row and step names 2 distinct experts; within the rows of one index of ep, over all 4 steps, no expert is named more than 12 times, and in every draw some expert is named exactly 12 times there. `lengths`: some row uses all 2048 cached positions.
All inputs are finite; a program needn't handle non-finite values.
Results may differ from a plain program's by a relative error of at most 0.014.
Values may be sent and summed in bfloat16 or wider, within the bound.
A program may use at most 64 MiB of HBM per device.

v0:
```python
import jax
import jax.numpy as jnp
from jax import lax
from jax.sharding import PartitionSpec as P

LAT = 512


score_scale = 192.0 ** (-0.5)
route_scale = 2.5
norm_eps = 1e-06


def attend_block(queries, kv_cache, new_kv, lengths):
    rows_here, steps_here, heads_here, kv_width = queries.shape
    positions = kv_cache.shape[1]
    cached = (
        jnp.einsum("rshk,rck->rshc", queries, kv_cache, preferred_element_type=jnp.float32)
        * score_scale
    )
    recent = (
        jnp.einsum("rshk,rjk->rshj", queries, new_kv, preferred_element_type=jnp.float32)
        * score_scale
    )
    cache_live = lax.broadcasted_iota(jnp.int32, (rows_here, positions), 1) < lengths[:, None]
    causal = lax.broadcasted_iota(jnp.int32, (steps_here, steps_here), 1) <= lax.broadcasted_iota(
        jnp.int32, (steps_here, steps_here), 0
    )
    cached = jnp.where(cache_live[:, None, None, :], cached, -1e30)
    recent = jnp.where(causal[None, :, None, :], recent, -1e30)
    highest = jnp.maximum(cached.max(-1), recent.max(-1))[..., None]
    cached_exp = jnp.exp(cached - highest)
    recent_exp = jnp.exp(recent - highest)
    denominator = cached_exp.sum(-1, keepdims=True) + recent_exp.sum(-1, keepdims=True)
    cached_prob = (cached_exp / denominator).astype(jnp.bfloat16)
    recent_prob = (recent_exp / denominator).astype(jnp.bfloat16)
    combined = jnp.einsum(
        "rshc,rck->rshk", cached_prob, kv_cache, preferred_element_type=jnp.float32
    )
    combined = combined + jnp.einsum(
        "rshj,rjk->rshk", recent_prob, new_kv, preferred_element_type=jnp.float32
    )
    return combined[..., :LAT].astype(jnp.bfloat16)


def on_device(
    hidden_in,
    queries,
    kv_cache,
    new_kv,
    lengths,
    expert_ids,
    value_up,
    out_proj,
    norm_gain,
    router,
    expert_in,
    expert_out,
    shared_in,
    shared_out,
):
    rows_here = hidden_in.shape[0]
    steps_here = hidden_in.shape[1]
    model_width = hidden_in.shape[2]
    latent_out = attend_block(queries, kv_cache, new_kv, lengths)
    by_head = lax.all_to_all(latent_out, ("ep", "tp"), split_axis=2, concat_axis=0, tiled=True)
    head_vals = jnp.einsum(
        "rshl,hlv->rshv", by_head, value_up, preferred_element_type=jnp.float32
    ).astype(jnp.bfloat16)
    attention = lax.psum_scatter(
        jnp.einsum("rshv,hvd->rsd", head_vals, out_proj, preferred_element_type=jnp.float32),
        ("ep", "tp"),
        scatter_dimension=0,
        tiled=True,
    )
    residual = hidden_in.astype(jnp.float32) + attention
    mean_square = jnp.mean(residual * residual, axis=-1, keepdims=True)
    normed = (residual * lax.rsqrt(mean_square + norm_eps) * norm_gain.astype(jnp.float32)).astype(
        jnp.bfloat16
    )
    block_items = lax.all_gather(
        normed.reshape(rows_here * steps_here, model_width), "tp", axis=0, tiled=True
    )
    item_count = block_items.shape[0]
    expert_count = router.shape[1]
    capacity = 3 * item_count // 4
    affinity = jax.nn.sigmoid(jnp.dot(block_items, router, preferred_element_type=jnp.float32))
    picked = expert_ids.reshape(item_count, expert_ids.shape[2])
    expert_iota = lax.broadcasted_iota(jnp.int32, (1, 1, expert_count), 2)
    chosen = jnp.sum((picked[:, :, None] == expert_iota).astype(jnp.int32), axis=1)
    scored = chosen.astype(jnp.float32) * affinity
    gate_weight = route_scale * scored / jnp.sum(scored, axis=-1, keepdims=True)
    slot_index = jnp.cumsum(chosen, axis=0) - chosen
    slot_iota = lax.broadcasted_iota(jnp.int32, (1, 1, capacity), 2)
    slot_hit = (slot_index[:, :, None] == slot_iota) & (chosen[:, :, None] > 0)
    outgoing = jnp.einsum(
        "mux,mt->uxt",
        slot_hit.astype(jnp.bfloat16),
        block_items,
        preferred_element_type=jnp.float32,
    ).astype(jnp.bfloat16)
    arrived = lax.all_to_all(outgoing, "ep", split_axis=0, concat_axis=0, tiled=True)
    gate_part = jnp.einsum(
        "scd,df->scf", arrived, expert_in[0, 0], preferred_element_type=jnp.float32
    )
    up_part = jnp.einsum(
        "scd,df->scf", arrived, expert_in[0, 1], preferred_element_type=jnp.float32
    )
    activated = (jax.nn.silu(gate_part) * up_part).astype(jnp.bfloat16)
    produced = jnp.einsum(
        "scf,fd->scd", activated, expert_out[0], preferred_element_type=jnp.float32
    )
    returned_slots = lax.all_to_all(
        produced.astype(jnp.bfloat16), "ep", split_axis=0, concat_axis=0, tiled=True
    ).astype(produced.dtype)
    combine = jnp.where(slot_hit, gate_weight[:, :, None], 0.0)
    routed_part = jnp.einsum(
        "jpo,pos->js",
        combine,
        returned_slots,
        precision=lax.Precision.HIGHEST,
        preferred_element_type=jnp.float32,
    )
    shared_gate = jnp.dot(block_items, shared_in[0], preferred_element_type=jnp.float32)
    shared_up = jnp.dot(block_items, shared_in[1], preferred_element_type=jnp.float32)
    shared_act = (jax.nn.silu(shared_gate) * shared_up).astype(jnp.bfloat16)
    shared_part = jnp.dot(shared_act, shared_out, preferred_element_type=jnp.float32)
    expert_sum = lax.psum_scatter(
        (routed_part + shared_part).astype(jnp.bfloat16), "tp", scatter_dimension=0, tiled=True
    ).astype(jnp.float32)
    layer_out = (residual + expert_sum.reshape(rows_here, steps_here, model_width)).astype(
        jnp.bfloat16
    )
    return layer_out


def solution(mesh):
    in_specs = (
        P(("groups", "ep", "tp"), None, None),
        P(("groups", "ep", "tp"), None, None, None),
        P(("groups", "ep", "tp"), None, None),
        P(("groups", "ep", "tp"), None, None),
        P(("groups", "ep", "tp")),
        P(("groups", "ep"), None, None),
        P(("ep", "tp"), None, None),
        P(("ep", "tp"), None, None),
        P(),
        P(),
        P("ep", None, None, "tp"),
        P("ep", "tp", None),
        P(None, None, "tp"),
        P("tp", None),
    )
    out_specs = P(("groups", "ep", "tp"), None, None)
    return jax.shard_map(
        on_device, mesh=mesh, in_specs=in_specs, out_specs=out_specs, check_vma=False
    )
```

profile of v0, /device:TPU:0, one launch (start us, length us, event | category | flops | bytes accessed | tf_op | source)
XLA Modules:
  0.0 233.5 jit_solution(7596553311977979096)
XLA Ops:
  6.5 0.0 copy-start
  6.5 0.0 copy-start.1
  6.5 0.0 all-reduce.5.cloned.1.call-start
  7.4 0.8 copy-done
  8.2 3.2 %fusion.6 = (f32[4,128]{1,0:T(4,128)S(1)}, f32[4,128,2048]{2,1,0:T(8,128)S(1)}) fusion(pred[2048]{0:T(1024)(128)(4,1)S(1)} %iota_compare_fusion.1, bf16[1,2048,576]{1,2,0:T(8,128)(2,1)S(1)} %copy-done, bf16[1,4,128,576]{2,3,1,0:T(8,128)(2,1)} %param.15), kind=kOutput, calls=%fused_computation.11 | convolution fusion | flops 1211104768 | bytes 7147520 | tf_op jit(solution)/shard_map/rshk,rck->rshc/dot_general | solution.py:18
  11.4 0.0 copy-done.1
  11.4 0.0 copy-done.3
  11.4 0.2 fusion.97
  11.6 0.9 fusion.14
  12.6 1.7 fusion.15
  14.3 0.4 fusion.27
  14.7 0.4 copy.40
  15.1 22.9 %all_to_all.28 = bf16[1,4,128,512]{3,1,0,2:T(4,128)(2,1)} all-to-all(bf16[1,4,128,512]{3,1,0,2:T(4,128)(2,1)S(1)} %copy.40), channel_id=1, replica_groups=mesh['groups'=2,'ep'=4,'tp'=4] {'ep','tp'}, dimensions={2} | all-to-all | bytes 1048576 | tf_op jit(solution)/shard_map/all_to_all | solution.py:66
  38.1 5.3 %fusion.2 = f32[16,4,3584]{2,0,1:T(8,128)S(1)} fusion(bf16[8,128,3584]{2,1,0:T(8,128)(2,1)} %param.21, bf16[8,512,128]{2,1,0:T(8,128)(2,1)} %param.20, bf16[1,4,16,8,512]{4,1,3,2,0:T(4,128)(2,1)} %bitcast.112), kind=kOutput, calls=%fused_computation.2 | convolution fusion | flops 536936448 | bytes 9830400 | tf_op jit(solution)/shard_map/rshv,hvd->rsd/dot_general | solution.py:71
  43.4 0.0 copy-start.6
  43.4 1.6 copy.43
  45.0 0.0 all-reduce.5.cloned.1.call-update
  45.0 0.0 copy-done.4
  45.0 0.0 copy-done.5
  45.0 0.1 eq.28
  45.1 0.1 copy.45
  45.3 0.1 copy.47
  45.4 0.0 copy-done.8
  45.4 0.6 dynamic-slice
  46.0 89.8 %all-reduce.5.cloned.1.call-done = f32[16,4,3584]{2,1,0:T(4,128)} async-done(((f32[16,4,3584]{2,1,0:T(4,128)}), f32[16,4,3584]{2,1,0:T(4,128)}) %all-reduce.5.cloned.1.call-update) | async-done | bytes 917520
  135.8 0.0 copy-done.2
  135.8 1.5 multiply_reduce_fusion
  137.3 1.5 multiply_convert_fusion
  138.8 14.4 %all-gather = bf16[1,16,3584]{2,0,1:T(2,128)(2,1)S(1)} all-gather(bf16[1,4,3584]{2,0,1:T(2,128)(2,1)S(1)} %copy.48), channel_id=2, replica_groups=mesh['groups'=2,'ep'=4,'tp'=4] {'tp'}, dimensions={1}, use_global_device_ids=true | all-gather | bytes 143360 | tf_op jit(solution)/shard_map/all_gather | solution.py:81
  153.3 1.2 convolution_convert_fusion.1
  154.5 3.5 %all-to-all-start.1 = ((bf16[4,12,3584]{2,1,0:T(8,128)(2,1)}), bf16[4,12,3584]{2,1,0:T(8,128)(2,1)S(1)}, u32[]{:S(2)}, u32[]{:S(2)}) async-start(bf16[4,12,3584]{2,1,0:T(8,128)(2,1)} %convolution_convert_fusion.1), calls=%async_computation.1 | async-start | bytes 917504 | tf_op jit(solution)/shard_map/all_to_all | solution.py:102
  157.9 0.0 copy-done.6
  157.9 0.2 fusion.98
  158.1 7.9 %all-to-all-done.1 = bf16[4,12,3584]{2,1,0:T(8,128)(2,1)S(1)} async-done(((bf16[4,12,3584]{2,1,0:T(8,128)(2,1)}), bf16[4,12,3584]{2,1,0:T(8,128)(2,1)S(1)}, u32[]{:S(2)}, u32[]{:S(2)}) %all-to-all-start.1) | async-done | bytes 344096 | tf_op jit(solution)/shard_map/all_to_all | solution.py:102
  166.0 2.8 %fusion.9 = f32[4,12,512]{2,1,0:T(8,128)S(1)} fusion(bf16[4,12,3584]{2,1,0:T(8,128)(2,1)S(1)} %all-to-all-done.1, bf16[1,2,3584,512]{3,2,1,0:T(8,128)(2,1)} %param.24), kind=kOutput, calls=%fused_computation.14 | convolution fusion | flops 176160768 | bytes 4112384 | tf_op jit(solution)/shard_map/scd,df->scf/dot_general | solution.py:103
  168.8 5.4 %convolution_convert_fusion = bf16[4,12,3584]{2,1,0:T(8,128)(2,1)} fusion(bf16[1,512,3584]{2,1,0:T(8,128)(2,1)} %param.25, bf16[4,12,3584]{2,1,0:T(8,128)(2,1)S(1)} %all-to-all-done.1, bf16[1,2,3584,512]{3,2,1,0:T(8,128)(2,1)} %param.24, f32[4,12,512]{2,1,0:T(8,128)S(1)} %fusion.9), kind=kOutput, calls=%fused_computation.3 | convolution fusion | flops 352641024 | bytes 8126464 | tf_op jit(solution)/shard_map/scf,fd->scd/dot_general | solution.py:110
  174.2 3.5 %all-to-all-start.2 = ((bf16[4,12,3584]{2,1,0:T(8,128)(2,1)}), bf16[4,12,3584]{2,1,0:T(8,128)(2,1)S(1)}, u32[]{:S(2)}, u32[]{:S(2)}) async-start(bf16[4,12,3584]{2,1,0:T(8,128)(2,1)} %convolution_convert_fusion), calls=%async_computation.2 | async-start | bytes 917504 | tf_op jit(solution)/shard_map/all_to_all | solution.py:113
  177.7 0.0 copy-start.7
  177.7 0.0 all-reduce.7.cloned.1.call-start
  177.7 1.8 fusion.22
  179.6 6.2 %all-to-all-done.2 = bf16[4,12,3584]{2,1,0:T(8,128)(2,1)S(1)} async-done(((bf16[4,12,3584]{2,1,0:T(8,128)(2,1)}), bf16[4,12,3584]{2,1,0:T(8,128)(2,1)S(1)}, u32[]{:S(2)}, u32[]{:S(2)}) %all-to-all-start.2) | async-done | bytes 344096 | tf_op jit(solution)/shard_map/all_to_all | solution.py:113
  185.8 0.7 convolution_bitcast_fusion
  186.5 3.9 %fusion.5 = bf16[16,3584]{1,0:T(8,128)(2,1)} fusion(f32[16,3584]{1,0:T(8,128)S(1)} %convolution_bitcast_fusion, bf16[256,3584]{1,0:T(8,128)(2,1)} %param.27, bf16[2,3584,256]{2,1,0:T(8,128)(2,1)} %param.26, bf16[1,16,3584]{2,1,0:T(8,128)(2,1)S(1)} %copy.54, f32[16,256]{1,0:T(8,128)S(1)} %fusion.22), kind=kOutput, calls=%fused_computation.7 | convolution fusion | flops 58859520 | bytes 4145152 | tf_op jit(solution)/shard_map/dot_general | solution.py:127
  190.3 0.0 all-reduce.7.cloned.1.call-update
  190.4 0.0 copy-done.7
  190.4 0.6 dynamic-slice.2
  191.6 33.0 %all-reduce.7.cloned.1.call-done = bf16[16,3584]{1,0:T(8,128)(2,1)} async-done(((bf16[16,3584]{1,0:T(8,128)(2,1)}), bf16[16,3584]{1,0:T(8,128)(2,1)}) %all-reduce.7.cloned.1.call-update) | async-done | bytes 114704
  224.6 2.1 fusion.70
  (21 shorter events, 0.2 us)
Async XLA Ops:
  6.5 1.7 copy-start
  6.5 4.8 %copy-start.1 = (bf16[1,4,128,576]{2,3,1,0:T(8,128)(2,1)S(1)}, bf16[1,4,128,576]{2,3,1,0:T(8,128)(2,1)}, u32[]{:S(2)}) copy-start(bf16[1,4,128,576]{2,3,1,0:T(8,128)(2,1)} %param.15) | copy-start | bytes 1769476
  6.5 4.8 %copy-start.3 = (bf16[1,4,576]{2,1,0:T(4,128)(2,1)S(1)}, bf16[1,4,576]{2,1,0:T(4,128)(2,1)}, u32[]{:S(2)}) copy-start(bf16[1,4,576]{2,1,0:T(4,128)(2,1)} %param.17) | copy-start | bytes 13828
  6.5 129.2 %all-reduce.5.cloned.1.call-start = ((), (), s32[]{:S(2)}) async-start(), calls=%async_computation.3 | async-start | bytes 1835008
  38.1 6.9 %copy-start.4 = (bf16[3584]{0:T(1024)(128)(2,1)S(1)}, bf16[3584]{0:T(1024)(128)(2,1)}, u32[]{:S(2)}) copy-start(bf16[3584]{0:T(1024)(128)(2,1)} %param.22) | copy-start | bytes 21508
  38.1 7.0 %copy-start.5 = (s32[4,4,2]{1,2,0:T(2,128)S(1)}, s32[4,4,2]{1,2,0:T(2,128)}, u32[]{:S(2)}) copy-start(s32[4,4,2]{1,2,0:T(2,128)} %param.19) | copy-start | bytes 388
  38.1 7.3 %copy-start.8 = (u32[32]{0:T(128)S(1)}, u32[32]{0:T(128)}, u32[]{:S(2)}) copy-start(u32[32]{0:T(128)} %constant.40) | copy-start | bytes 388
  38.1 97.7 %copy-start.2 = (bf16[1,4,3584]{2,1,0:T(4,128)(2,1)S(1)}, bf16[1,4,3584]{2,1,0:T(4,128)(2,1)}, u32[]{:S(2)}) copy-start(bf16[1,4,3584]{2,1,0:T(4,128)(2,1)} %param.14) | copy-start | bytes 86020
  43.4 114.5 %copy-start.6 = (bf16[3584,4]{0,1:T(4,128)(2,1)S(1)}, bf16[3584,4]{0,1:T(4,128)(2,1)}, u32[]{:S(2)}) copy-start(bf16[3584,4]{0,1:T(4,128)(2,1)} %param.23) | copy-start | bytes 86020
  154.5 11.6 %all-to-all-start.1 = ((bf16[4,12,3584]{2,1,0:T(8,128)(2,1)}), bf16[4,12,3584]{2,1,0:T(8,128)(2,1)S(1)}, u32[]{:S(2)}, u32[]{:S(2)}) async-start(bf16[4,12,3584]{2,1,0:T(8,128)(2,1)} %convolution_convert_fusion.1), calls=%async_computation.1 | async-start | bytes 917504 | tf_op jit(solution)/shard_map/all_to_all | solution.py:102
  174.2 11.6 %all-to-all-start.2 = ((bf16[4,12,3584]{2,1,0:T(8,128)(2,1)}), bf16[4,12,3584]{2,1,0:T(8,128)(2,1)S(1)}, u32[]{:S(2)}, u32[]{:S(2)}) async-start(bf16[4,12,3584]{2,1,0:T(8,128)(2,1)} %convolution_convert_fusion), calls=%async_computation.2 | async-start | bytes 917504 | tf_op jit(solution)/shard_map/all_to_all | solution.py:113
  177.7 12.7 %copy-start.7 = (u32[32]{0:T(128)S(1)}, u32[32]{0:T(128)}, u32[]{:S(2)}) copy-start(u32[32]{0:T(128)} %constant.44) | copy-start | bytes 388
  177.7 46.9 %all-reduce.7.cloned.1.call-start = ((), (), s32[]{:S(2)}) async-start(), calls=%async_computation.4 | async-start | bytes 229376
Sparse Core Ops, SparseCore 0:
  45.1 90.5 all-reduce.4
  190.5 34.0 all-reduce.6
where the time goes:
time: 234 us
  waiting for transfers between devices  137 us (59%)
  blocking collectives  37.4 us (16%)
  matrix products  26.6 us (11%)
  between operations  15.1 us (6%)
  starting transfers between devices  6.97 us (3%)
  other arithmetic  6.16 us (3%)
  local copies, waits for them, and re-layouts  4.37 us (2%)
    unnamed x4, waiting for transfers between devices  123 us
    all_to_all x1, blocking collectives, on_device(): lax.all_to_all(latent_out, ('ep', 'tp'), split_axis=2, concat_axis=0, til...  22.9 us
    all_gather x1, blocking collectives, on_device(): lax.all_gather(normed.reshape(rows_here * steps_here, model_width), 'tp',...  14.4 us
    all_to_all x1, waiting for transfers between devices, on_device(): lax.all_to_all(outgoing, 'ep', split_axis=0, concat_axis=0, tiled=True)  7.92 us
    all_to_all x1, waiting for transfers between devices, on_device(): lax.all_to_all(produced.astype(jnp.bfloat16), 'ep', split_axis=0, concat_...  6.2 us
    dot_general x1, matrix products, on_device(): jnp.einsum('scf,fd->scd', activated, expert_out[0], preferred_element_typ...  5.4 us
    dot_general x1, matrix products, on_device(): jnp.einsum('rshv,hvd->rsd', head_vals, out_proj, preferred_element_type=j...  5.31 us
  transfers between devices with their start and end apart: 4, of which 4 were waited for; matrix products, arithmetic and copies ran while one was open for 2% of the time, Pallas kernels for 0%

commit v1 on v0

v1 whole, which is shorter than its diff:
```python
import functools

import jax
import jax.numpy as jnp
from jax import lax
from jax.experimental import pallas as pl
from jax.experimental.pallas import tpu as pltpu
from jax.sharding import PartitionSpec as P

score_scale = 192.0 ** (-0.5)
route_scale = 2.5
norm_eps = 1e-06
MESH = pl.DeviceIdType.MESH
f32, bf16 = jnp.float32, jnp.bfloat16


def mm(a, b):
    return jnp.dot(a, b, preferred_element_type=f32)


def mm_nt(a, b):
    return lax.dot_general(a, b, (((1,), (1,)), ((), ())), preferred_element_type=f32)


def log2(n):
    assert n & (n - 1) == 0
    return n.bit_length() - 1


def iota2(shape, dim):
    return lax.broadcasted_iota(jnp.int32, shape, dim)


def onehot(target, shape):
    return jnp.where(iota2(shape, 1) == target, 1.0, 0.0).astype(bf16)


def layer_kernel(
    ep,
    tp,
    steps,
    heads,
    rp,
    lat,
    q_chunk,
    len_ref,
    hid_ref,
    gain_ref,
    chosen_ref,
    router_ref,
    q_hbm,
    kv_hbm,
    new_hbm,
    up_hbm,
    op_hbm,
    ein_hbm,
    eout_hbm,
    sin_hbm,
    sout_hbm,
    out_ref,
    q_v,
    kv_v,
    new_v,
    up_v,
    op_v,
    ein_v,
    eout_v,
    sin_v,
    sout_v,
    lat_send,
    lat_recv,
    vals_v,
    b_send,
    b_recv,
    t_send,
    t_recv,
    n_all,
    x_v,
    x_own,
    sh_v,
    f_send,
    f_recv,
    u_send,
    u_recv,
    ch_all,
    w_sem,
    ch_ss,
    ch_rs,
    a_ss,
    a_rs,
    b_ss,
    b_rs,
    t_ss,
    t_rs,
    c_ss,
    c_rs,
    d_ss,
    d_rs,
    f_ss,
    f_rs,
    u_ss,
    u_rs,
):
    my_ep, my_tp = lax.axis_index("ep"), lax.axis_index("tp")
    n = ep * tp
    me = my_ep * tp + my_tp
    pack = 16 // steps
    items = n * steps
    ep_items = tp * steps
    width = out_ref.shape[1]

    loads = [
        pltpu.make_async_copy(src, dst, w_sem.at[i])
        for i, (src, dst) in enumerate(
            [
                (q_hbm, q_v),
                (kv_hbm, kv_v),
                (new_hbm, new_v),
                (up_hbm, up_v),
                (op_hbm, op_v),
                (sin_hbm, sin_v),
                (sout_hbm, sout_v),
                (ein_hbm, ein_v),
                (eout_hbm, eout_v),
            ]
        )
    ]
    for load in loads:
        load.start()

    def dev(d):
        return {"ep": d // tp, "tp": d % tp}

    def ep_peer(o):
        return lax.rem(my_ep + o, ep)

    def tp_peer(o):
        return lax.rem(my_tp + o, tp)

    def remote(src, dst, ss, rs, where):
        return pltpu.make_async_remote_copy(
            src_ref=src, dst_ref=dst, send_sem=ss, recv_sem=rs, device_id=where, device_id_type=MESH
        )

    barrier = pltpu.get_barrier_semaphore()

    @pl.loop(1, n)
    def _(o):
        pl.semaphore_signal(
            barrier, inc=1, device_id=dev(lax.rem(me + o, n)), device_id_type=MESH
        )

    pl.semaphore_wait(barrier, n - 1)

    def chosen_copy(src, e):
        return remote(ch_all.at[my_ep], ch_all.at[src], ch_ss.at[e], ch_rs.at[src], {"ep": e})

    ch_all[my_ep] = chosen_ref[...]
    for o in range(1, ep):
        chosen_copy(my_ep, ep_peer(o)).start()

    def latent_copy(slot, d):
        return remote(lat_send.at[d], lat_recv.at[slot], a_ss.at[d], a_rs.at[slot], dev(d))

    for load in loads[:3]:
        load.wait()
    length = len_ref[0]
    dests = q_chunk // rp

    @pl.loop(0, n // dests)
    def _(c):
        q = q_v[pl.ds(c * dests, dests)].reshape(q_chunk, q_v.shape[2])
        kv = kv_v[...]
        new = new_v[...]
        cached = mm_nt(q, kv) * score_scale
        recent = mm_nt(q, new) * score_scale
        cached = jnp.where(iota2(cached.shape, 1) < length, cached, -1e30)
        row = iota2(recent.shape, 0) & (rp - 1)
        step = jnp.minimum(row >> log2(heads), steps - 1)
        recent = jnp.where(iota2(recent.shape, 1) <= step, recent, -1e30)
        highest = jnp.maximum(
            jnp.max(cached, axis=1, keepdims=True), jnp.max(recent, axis=1, keepdims=True)
        )
        cached = jnp.exp(cached - highest)
        recent = jnp.exp(recent - highest)
        total = jnp.sum(cached, axis=1, keepdims=True) + jnp.sum(recent, axis=1, keepdims=True)
        mixed = mm(cached.astype(bf16), kv[:, :lat]) + mm(recent.astype(bf16), new[:, :lat])
        lat_send[pl.ds(c * dests, dests)] = (mixed / total).astype(bf16).reshape(dests, rp, lat)

        @pl.loop(0, dests)
        def _(j):
            d = c * dests + j

            @pl.when(d != me)
            def _():
                latent_copy(me, d).start()

    lat_recv[me] = lat_send[me]
    loads[3].wait()
    loads[4].wait()

    @pl.loop(1, n)
    def _(o):
        d = lax.rem(me + o, n)
        latent_copy(d, d).wait_recv()

    shape = (heads * items, n * rp)
    r = iota2((shape[0], 1), 0)
    item = r & (items - 1)
    target = (
        (item >> log2(steps)) * rp + (item & (steps - 1)) * heads + (r >> log2(items))
    )
    by_head = mm(onehot(target, shape), lat_recv[...].reshape(n * rp, lat)).astype(bf16)
    vh = up_v.shape[2]
    for h in range(heads):
        vals_v[:, h * vh : (h + 1) * vh] = mm(
            by_head[h * items : (h + 1) * items], up_v[h]
        ).astype(bf16)

    def rs_copy(send, recv, ss, rs, k, slot, e):
        return remote(send.at[k, e], recv.at[k, slot], ss.at[k, e], rs.at[k, slot], {"ep": e})

    def tp_copy(send, recv, ss, rs, slot, t):
        return remote(send.at[t], recv.at[slot], ss.at[t], rs.at[slot], {"tp": t})

    def scatter_sum(part, extra, send, recv, ss, rs, send2, recv2, ss2, rs2):
        for k in range(pack):
            send[k] = part(k).astype(bf16).reshape(ep, ep_items, width)
            for o in range(1, ep):
                rs_copy(send, recv, ss, rs, k, my_ep, ep_peer(o)).start()
            recv[k, my_ep] = send[k, my_ep]
        sums = []
        for k in range(pack):
            for o in range(1, ep):
                rs_copy(send, recv, ss, rs, k, ep_peer(o), ep_peer(o)).wait_recv()
            total = jnp.sum(recv[k].astype(f32), axis=0)
            if extra is not None:
                total = total + extra(k)
            sums.append(total.astype(bf16))
        stacked = jnp.concatenate(sums, axis=0)
        r = iota2((tp * 16, 1), 0)
        target = (
            ((r & 15) >> log2(steps)) * ep_items + (r >> 4) * steps + (r & (steps - 1))
        )
        turned = mm(onehot(target, (tp * 16, pack * ep_items)), stacked).astype(bf16)
        send2[...] = turned.reshape(tp, 16, width)
        for o in range(1, tp):
            tp_copy(send2, recv2, ss2, rs2, my_tp, tp_peer(o)).start()
        recv2[my_tp] = send2[my_tp]
        for o in range(1, tp):
            tp_copy(send2, recv2, ss2, rs2, tp_peer(o), tp_peer(o)).wait_recv()
        return jnp.sum(recv2[...].astype(f32), axis=0)

    vals = vals_v[...]
    attention = scatter_sum(
        lambda k: mm(vals, op_v[:, k * width : (k + 1) * width]),
        None,
        b_send,
        b_recv,
        b_ss,
        b_rs,
        t_send,
        t_recv,
        t_ss,
        t_rs,
    )
    residual = hid_ref[...].astype(f32) + attention
    same = jnp.where(
        (iota2((16, 16), 0) & (steps - 1)) == (iota2((16, 16), 1) & (steps - 1)), 1.0, 0.0
    )
    squares = jnp.dot(
        same, residual * residual, precision=lax.Precision.HIGHEST, preferred_element_type=f32
    )
    mean_square = jnp.sum(squares, axis=1, keepdims=True) / (pack * width)
    normed = residual * lax.rsqrt(mean_square + norm_eps) * gain_ref[...].astype(f32)
    n_all[my_ep, my_tp] = normed.astype(bf16)

    def c_copy(slot, t):
        return remote(
            n_all.at[my_ep, my_tp], n_all.at[my_ep, slot], c_ss.at[t], c_rs.at[slot], {"tp": t}
        )

    def d_copy(t, slot, e):
        return remote(
            n_all.at[my_ep, t], n_all.at[slot, t], d_ss.at[t, e], d_rs.at[t, slot], {"ep": e}
        )

    for o in range(1, tp):
        c_copy(my_tp, tp_peer(o)).start()
    for o in range(1, ep):
        d_copy(my_tp, my_ep, ep_peer(o)).start()
    for p in range(1, tp):
        c_copy(tp_peer(p), tp_peer(p)).wait_recv()
        for o in range(1, ep):
            d_copy(tp_peer(p), my_ep, ep_peer(o)).start()

    def unpack(blocks, count, into):
        m = count * steps
        r = iota2((pack * m, 1), 0)
        item = r & (m - 1)
        target = (
            (item >> log2(steps)) * 16 + (r >> log2(m)) * steps + (item & (steps - 1))
        )
        flat = mm(onehot(target, (pack * m, count * 16)), blocks).astype(bf16)
        for k in range(pack):
            into[:, k * width : (k + 1) * width] = flat[k * m : (k + 1) * m]

    unpack(n_all[my_ep].reshape(tp * 16, width), tp, x_own)
    loads[5].wait()
    loads[6].wait()
    xo = x_own[...]
    shared_act = (jax.nn.silu(mm(xo, sin_v[0])) * mm(xo, sin_v[1])).astype(bf16)
    sh_v[...] = mm(shared_act, sout_v[...])
    loads[7].wait()
    loads[8].wait()
    for o in range(1, ep):
        chosen_copy(ep_peer(o), ep_peer(o)).wait_recv()
    for p in range(tp):
        for o in range(1, ep):
            d_copy(tp_peer(p), ep_peer(o), ep_peer(o)).wait_recv()

    unpack(n_all[...].reshape(n * 16, width), n, x_v)
    x = x_v[...]
    affinity = jax.nn.sigmoid(mm_nt(x, router_ref[...]))
    chosen = ch_all[...].reshape(items, ch_all.shape[2])[:, : affinity.shape[1]]
    scored = chosen * affinity
    mine = jnp.where(iota2(scored.shape, 1) == my_ep, scored, 0.0)
    gate = (
        route_scale
        * jnp.sum(mine, axis=1, keepdims=True)
        / jnp.sum(scored, axis=1, keepdims=True)
    )
    act = (jax.nn.silu(mm(x, ein_v[0])) * mm(x, ein_v[1])).astype(bf16)
    expert_sum = scatter_sum(
        lambda k: mm(act, eout_v[:, k * width : (k + 1) * width]) * gate,
        lambda k: sh_v[:, k * width : (k + 1) * width],
        f_send,
        f_recv,
        f_ss,
        f_rs,
        u_send,
        u_recv,
        u_ss,
        u_rs,
    )
    out_ref[...] = (residual + expert_sum).astype(bf16)

    @pl.loop(1, n)
    def _(o):
        d = lax.rem(me + o, n)
        latent_copy(me, d).wait_send()

    for o in range(1, ep):
        e = ep_peer(o)
        chosen_copy(my_ep, e).wait_send()
        for k in range(pack):
            rs_copy(b_send, b_recv, b_ss, b_rs, k, my_ep, e).wait_send()
            rs_copy(f_send, f_recv, f_ss, f_rs, k, my_ep, e).wait_send()
        for p in range(tp):
            d_copy(tp_peer(p), my_ep, e).wait_send()
    for o in range(1, tp):
        t = tp_peer(o)
        tp_copy(t_send, t_recv, t_ss, t_rs, my_tp, t).wait_send()
        tp_copy(u_send, u_recv, u_ss, u_rs, my_tp, t).wait_send()
        c_copy(my_tp, t).wait_send()


def on_device(
    ep,
    tp,
    hidden_in,
    queries,
    kv_cache,
    new_kv,
    lengths,
    expert_ids,
    value_up,
    out_proj,
    norm_gain,
    router,
    expert_in,
    expert_out,
    shared_in,
    shared_out,
):
    n = ep * tp
    rows, steps, d = hidden_in.shape
    heads, lat, vh = value_up.shape
    kvw = queries.shape[3]
    ctx = kv_cache.shape[1]
    assert rows == 1 and 16 % steps == 0
    pack = 16 // steps
    width = d // pack
    ep_items = tp * steps
    items = n * steps
    experts = router.shape[1]
    assert experts == ep
    rp = -(-steps * heads // 16) * 16
    q = queries[0].reshape(steps, n, heads, kvw).transpose(1, 0, 2, 3).reshape(n, steps * heads, kvw)
    q = jnp.pad(q, ((0, 0), (0, rp - steps * heads), (0, 0)))
    new = jnp.pad(new_kv[0], ((0, -steps % 16), (0, 0)))
    hid = hidden_in[0].reshape(steps, pack, width).transpose(1, 0, 2).reshape(16, width)
    gain = jnp.repeat(norm_gain.reshape(pack, width), steps, axis=0)
    e_pad = -(-experts // 16) * 16
    router_t = jnp.pad(router.T, ((0, e_pad - experts), (0, 0)))
    picked = expert_ids.reshape(ep_items, expert_ids.shape[2])
    lanes = lax.broadcasted_iota(jnp.int32, (1, 1, 128), 2)
    chosen = jnp.sum((picked[:, :, None] == lanes).astype(f32), axis=1)
    q_chunk = min(256, n * rp)
    hf = expert_in.shape[3]
    sf = shared_in.shape[2]

    vm, dma = pltpu.VMEM, pltpu.SemaphoreType.DMA
    scratch = [
        vm((n, rp, kvw), bf16),
        vm((ctx, kvw), bf16),
        vm(new.shape, bf16),
        vm(value_up.shape, bf16),
        vm((heads * vh, d), bf16),
        vm((2, d, hf), bf16),
        vm((hf, d), bf16),
        vm((2, d, sf), bf16),
        vm((sf, d), bf16),
        vm((n, rp, lat), bf16),
        vm((n, rp, lat), bf16),
        vm((items, heads * vh), bf16),
        vm((pack, ep, ep_items, width), bf16),
        vm((pack, ep, ep_items, width), bf16),
        vm((tp, 16, width), bf16),
        vm((tp, 16, width), bf16),
        vm((ep, tp, 16, width), bf16),
        vm((items, d), bf16),
        vm((ep_items, d), bf16),
        vm((ep_items, d), f32),
        vm((pack, ep, ep_items, width), bf16),
        vm((pack, ep, ep_items, width), bf16),
        vm((tp, 16, width), bf16),
        vm((tp, 16, width), bf16),
        vm((ep, ep_items, 128), f32),
        dma((9,)),
        dma((ep,)),
        dma((ep,)),
        dma((n,)),
        dma((n,)),
        dma((pack, ep)),
        dma((pack, ep)),
        dma((tp,)),
        dma((tp,)),
        dma((tp,)),
        dma((tp,)),
        dma((tp, ep)),
        dma((tp, ep)),
        dma((pack, ep)),
        dma((pack, ep)),
        dma((tp,)),
        dma((tp,)),
    ]
    vmem = pl.BlockSpec(memory_space=pltpu.VMEM)
    hbm = pl.BlockSpec(memory_space=pl.ANY)
    out = pl.pallas_call(
        functools.partial(layer_kernel, ep, tp, steps, heads, rp, lat, q_chunk),
        out_shape=jax.ShapeDtypeStruct((16, width), bf16),
        in_specs=[pl.BlockSpec(memory_space=pltpu.SMEM)] + [vmem] * 4 + [hbm] * 9,
        out_specs=vmem,
        scratch_shapes=scratch,
        compiler_params=pltpu.CompilerParams(
            collective_id=0, has_side_effects=True, vmem_limit_bytes=60 * 2**20
        ),
        name="layer",
    )(
        lengths,
        hid,
        gain,
        chosen,
        router_t,
        q,
        kv_cache[0],
        new,
        value_up,
        out_proj.reshape(heads * vh, d),
        expert_in[0],
        expert_out[0],
        shared_in,
        shared_out,
    )
    return out.reshape(pack, steps, width).transpose(1, 0, 2).reshape(1, steps, d)


def solution(mesh):
    rows = ("groups", "ep", "tp")
    in_specs = (
        P(rows, None, None),
        P(rows, None, None, None),
        P(rows, None, None),
        P(rows, None, None),
        P(rows),
        P(("groups", "ep"), None, None),
        P(("ep", "tp"), None, None),
        P(("ep", "tp"), None, None),
        P(),
        P(),
        P("ep", None, None, "tp"),
        P("ep", "tp", None),
        P(None, None, "tp"),
        P("tp", None),
    )
    body = functools.partial(on_device, mesh.shape["ep"], mesh.shape["tp"])
    return jax.shard_map(
        body, mesh=mesh, in_specs=in_specs, out_specs=P(rows, None, None), check_vma=False
    )
```

time: 234 us -> 73.6 us (0.31)
  waiting for transfers between devices: 137 us -> 0 us
  Pallas kernels: 0 us -> 59.2 us
  blocking collectives: 37.4 us -> 0 us
  matrix products: 26.6 us -> 0 us
  between operations: 15.1 us -> 0.82 us
  local copies, waits for them, and re-layouts: 4.37 us -> 12.4 us
  starting transfers between devices: 6.97 us -> 0 us
  other arithmetic: 6.16 us -> 0.67 us
    unnamed x4 -> x0, waiting for transfers between devices: 123 us -> none
    pallas_call x0 -> x1, Pallas kernels: none -> 59.2 us  [on_device(): pl.pallas_call(functools.partial(layer_kernel, ep, tp, steps, heads, rp,...]
    dot_general x12 -> x0, matrix products: 26.6 us -> none  [the longest x1 5.4 us: on_device(): jnp.einsum('scf,fd->scd', activated, expert_out[0], preferred_element_typ...]
    all_to_all x1 -> x0, blocking collectives: 22.9 us -> none  [on_device(): lax.all_to_all(latent_out, ('ep', 'tp'), split_axis=2, concat_axis=0, til...]
    all_gather x1 -> x0, blocking collectives: 14.4 us -> none  [on_device(): lax.all_gather(normed.reshape(rows_here * steps_here, model_width), 'tp',...]
    all_to_all x2 -> x0, waiting for transfers between devices: 14.1 us -> none  [the longest x1 7.92 us: on_device(): lax.all_to_all(outgoing, 'ep', split_axis=0, concat_axis=0, tiled=True)]
    all_to_all x2 -> x0, starting transfers between devices: 6.93 us -> none  [the longest x1 3.46 us: on_device(): lax.all_to_all(outgoing, 'ep', split_axis=0, concat_axis=0, tiled=True)]
    reshape x0 -> x5, local copies, waits for them, and re-layouts: none -> 4.97 us  [the longest x1 1.37 us: on_device(): out.reshape(pack, steps, width).transpose(1, 0, 2).reshape(1, steps, d)]
  transfers between devices with their start and end apart: 4 -> 0, of which waited for: 4 -> 0; matrix products, arithmetic and copies ran while one was open for 2% -> 0% of each run, Pallas kernels for 0% -> 0%
where the time goes in v1:
time: 73.6 us; the launch traced here: 73.1 us
  Pallas kernels  59.2 us (80%)
  local copies, waits for them, and re-layouts  12.4 us (17%)
  between operations  0.82 us (1%)
    pallas_call x1, Pallas kernels, on_device(): pl.pallas_call(functools.partial(layer_kernel, ep, tp, steps, heads, rp,...  59.2 us
    unnamed x5, local copies, waits for them, and re-layouts  4.62 us

profile of v1, /device:TPU:0, one launch (start us, length us, event | category | flops | bytes accessed | tf_op | source)
XLA Modules:
  0.0 73.1 jit_solution(16852125833445058131)
XLA Ops:
  0.0 0.0 copy-start
  0.8 0.7 copy.29
  1.5 0.1 eq.15
  1.6 0.7 convert_reduce_fusion.chosen_ref
  2.3 0.7 reshape.23
  3.0 1.3 %pad.9.new_hbm = bf16[16,576]{1,0:T(8,128)(2,1)} pad(bf16[4,576]{1,0:T(4,128)(2,1)} %bitcast.27, bf16[]{:T(256)} %constant.4.clone.1), padding=0_12x0_0 | pad | bytes 23042 | tf_op jit(solution)/shard_map/jit(_pad)/pad | solution.py:401
  4.3 0.6 reshape.24.gain_ref
  4.9 1.4 %reshape.22.hid_ref = bf16[16,896]{1,0:T(8,128)(2,1)} reshape(bf16[4,4,896]{2,1,0:T(4,128)(2,1)} %bitcast.25) | data formatting | bytes 57344 | tf_op jit(solution)/shard_map/reshape | solution.py:402
  6.3 1.4 %pad.8.router_ref = bf16[16,3584]{1,0:T(8,128)(2,1)} pad(bf16[4,3584]{1,0:T(4,128)(2,1)} %bitcast.26, bf16[]{:T(256)} %constant.4.clone.1), padding=0_12x0_0 | pad | bytes 143362 | tf_op jit(solution)/shard_map/jit(_pad)/pad | solution.py:405
  7.7 1.4 %copy.30 = bf16[1,4,128,576]{3,2,1,0:T(8,128)(2,1)S(1)} copy(bf16[1,4,128,576]{2,3,1,0:T(8,128)(2,1)} %param.15) | data formatting | bytes 1179648 | tf_op args[1]
  9.0 0.9 %copy_bitcast_fusion.q_hbm = bf16[16,32,576]{2,1,0:T(8,128)(2,1)} fusion(bf16[1,4,128,576]{3,2,1,0:T(8,128)(2,1)S(1)} %copy.30), kind=kLoop, calls=%fused_computation | loop fusion | bytes 1179648 | tf_op jit(solution)/shard_map/reshape | solution.py:399
  9.9 0.0 copy-done
  9.9 2.6 %copy.32 = bf16[1,2048,576]{2,1,0:T(8,128)(2,1)} copy(bf16[1,2048,576]{1,2,0:T(8,128)(2,1)S(1)} %copy-done) | data formatting | bytes 4718592 | tf_op args[2]
  12.5 59.2 %layer.1 = bf16[16,896]{1,0:T(8,128)(2,1)} custom-call(s32[1]{0:T(128)S(6)} %copy.35.len_ref, bf16[16,896]{1,0:T(8,128)(2,1)} %reshape.22.hid_ref, bf16[16,896]{1,0:T(8,128)(2,1)} %reshape.24.gain_ref, f32[16,128]{1,0:T(8,128)} %convert_reduce_fusion.chosen_ref, bf16[16,3584]{1,0:T(8,128)(2,1)} %pad.8.router_ref, ...), custom_call_target="tpu_custom_call" | custom-call | tf_op jit(solution)/shard_map/layer/pallas_call | solution.py:460
  71.7 1.4 %reshape.27 = bf16[4,4,896]{2,1,0:T(4,128)(2,1)} reshape(bf16[16,896]{1,0:T(8,128)(2,1)} %layer.1) | data formatting | bytes 57344 | tf_op jit(solution)/shard_map/reshape | solution.py:486
  (1 shorter events, 0.0 us)
Async XLA Ops:
  0.0 9.9 %copy-start = (bf16[1,2048,576]{1,2,0:T(8,128)(2,1)S(1)}, bf16[1,2048,576]{1,2,0:T(8,128)(2,1)}, u32[]{:S(2)}) copy-start(bf16[1,2048,576]{1,2,0:T(8,128)(2,1)} %param.16) | copy-start | bytes 7077892

commit v2 on v1

--- a/solution.py
+++ b/solution.py
@@ -46,11 +46,11 @@
     len_ref,
     hid_ref,
     gain_ref,
-    chosen_ref,
+    ids_ref,
     router_ref,
+    new_v,
     q_hbm,
     kv_hbm,
-    new_hbm,
     up_hbm,
     op_hbm,
     ein_hbm,
@@ -60,7 +60,6 @@
     out_ref,
     q_v,
     kv_v,
-    new_v,
     up_v,
     op_v,
     ein_v,
@@ -107,7 +106,7 @@
     pack = 16 // steps
     items = n * steps
     ep_items = tp * steps
-    width = out_ref.shape[1]
+    width = out_ref.shape[1] // pack
 
     loads = [
         pltpu.make_async_copy(src, dst, w_sem.at[i])
@@ -115,7 +114,6 @@
             [
                 (q_hbm, q_v),
                 (kv_hbm, kv_v),
-                (new_hbm, new_v),
                 (up_hbm, up_v),
                 (op_hbm, op_v),
                 (sin_hbm, sin_v),
@@ -150,33 +148,60 @@
             barrier, inc=1, device_id=dev(lax.rem(me + o, n)), device_id_type=MESH
         )
 
-    pl.semaphore_wait(barrier, n - 1)
-
     def chosen_copy(src, e):
         return remote(ch_all.at[my_ep], ch_all.at[src], ch_ss.at[e], ch_rs.at[src], {"ep": e})
 
-    ch_all[my_ep] = chosen_ref[...]
-    for o in range(1, ep):
-        chosen_copy(my_ep, ep_peer(o)).start()
-
-    def latent_copy(slot, d):
-        return remote(lat_send.at[d], lat_recv.at[slot], a_ss.at[d], a_rs.at[slot], dev(d))
-
-    for load in loads[:3]:
+    shape = (ep_items, ch_all.shape[2])
+    row, lane = iota2(shape, 0), iota2(shape, 1)
+    chosen = jnp.zeros(shape, f32)
+    for i in range(ep_items):
+        for k in range(ids_ref.shape[1]):
+            hit = (row == i) & (lane == ids_ref[i // steps, k, i % steps])
+            chosen = chosen + jnp.where(hit, 1.0, 0.0)
+    ch_all[my_ep] = chosen
+
+    def owner(o):
+        return my_ep ^ lax.rem(o, ep), my_tp ^ (o // ep)
+
+    def latent_copy(o):
+        e, t = owner(o)
+        return remote(
+            lat_send.at[o], lat_recv.at[me], a_ss.at[o], a_rs.at[me], {"ep": e, "tp": t}
+        )
+
+    def latent_arrival(o):
+        e, t = owner(o)
+        d = e * tp + t
+        return remote(
+            lat_send.at[o], lat_recv.at[d], a_ss.at[o], a_rs.at[d], {"ep": e, "tp": t}
+        )
+
+    for load in loads[:2]:
         load.wait()
     length = len_ref[0]
     dests = q_chunk // rp
-
-    @pl.loop(0, n // dests)
-    def _(c):
-        q = q_v[pl.ds(c * dests, dests)].reshape(q_chunk, q_v.shape[2])
+    chunks = n // dests
+
+    def attend(c):
+        first = (chunks - 1 - c) * dests
+        row = iota2((q_chunk, 1), 0)
+        o = first + (row >> log2(rp))
+        within = row & (rp - 1)
+        step = within >> log2(heads)
+        e = my_ep ^ (o & (ep - 1))
+        t = my_tp ^ (o >> log2(ep))
+        head = (e * tp + t) * heads + (within & (heads - 1))
+        q = jnp.zeros((q_chunk, kv_v.shape[0]), f32)
+        for s in range(steps):
+            pick = onehot(jnp.where(step == s, head, -1), (q_chunk, q_v.shape[2]))
+            q = q + mm_nt(pick, q_v[s])
+        q = q.astype(bf16)
         kv = kv_v[...]
         new = new_v[...]
-        cached = mm_nt(q, kv) * score_scale
+        cached = mm(q, kv) * score_scale
         recent = mm_nt(q, new) * score_scale
         cached = jnp.where(iota2(cached.shape, 1) < length, cached, -1e30)
-        row = iota2(recent.shape, 0) & (rp - 1)
-        step = jnp.minimum(row >> log2(heads), steps - 1)
+        step = jnp.minimum(step, steps - 1)
         recent = jnp.where(iota2(recent.shape, 1) <= step, recent, -1e30)
         highest = jnp.maximum(
             jnp.max(cached, axis=1, keepdims=True), jnp.max(recent, axis=1, keepdims=True)
@@ -184,25 +209,38 @@
         cached = jnp.exp(cached - highest)
         recent = jnp.exp(recent - highest)
         total = jnp.sum(cached, axis=1, keepdims=True) + jnp.sum(recent, axis=1, keepdims=True)
-        mixed = mm(cached.astype(bf16), kv[:, :lat]) + mm(recent.astype(bf16), new[:, :lat])
-        lat_send[pl.ds(c * dests, dests)] = (mixed / total).astype(bf16).reshape(dests, rp, lat)
-
+        mixed = mm_nt(cached.astype(bf16), kv[:lat])
+        mixed = mixed + mm(recent.astype(bf16), new[:, :lat])
+        mixed = (mixed / total).astype(bf16).reshape(dests, rp, lat)
+        lat_send[pl.ds(first, dests)] = mixed
+
+    def send_block(c):
         @pl.loop(0, dests)
         def _(j):
-            d = c * dests + j
-
-            @pl.when(d != me)
+            o = (chunks - c) * dests - 1 - j
+
+            @pl.when(o > 0)
             def _():
-                latent_copy(me, d).start()
-
-    lat_recv[me] = lat_send[me]
+                latent_copy(o).start()
+
+    attend(0)
+    pl.semaphore_wait(barrier, n - 1)
+    send_block(0)
+    for o in range(1, ep):
+        chosen_copy(my_ep, ep_peer(o)).start()
+
+    @pl.loop(1, chunks)
+    def _(c):
+        attend(c)
+        send_block(c)
+
+    lat_recv[me] = lat_send[0]
+    loads[2].wait()
     loads[3].wait()
-    loads[4].wait()
 
     @pl.loop(1, n)
     def _(o):
-        d = lax.rem(me + o, n)
-        latent_copy(d, d).wait_recv()
+        latent_arrival(o).wait_recv()
 
     shape = (heads * items, n * rp)
     r = iota2((shape[0], 1), 0)
@@ -264,7 +302,16 @@
         t_ss,
         t_rs,
     )
-    residual = hid_ref[...].astype(f32) + attention
+    hidden = hid_ref[...].astype(f32)
+    gain = gain_ref[...].astype(f32).reshape(1, pack * width)
+
+    def columns(a, k):
+        return a[:, k * width : (k + 1) * width]
+
+    residual = attention + jnp.concatenate([columns(hidden, k) for k in range(pack)], axis=0)
+    gain = jnp.concatenate(
+        [jnp.broadcast_to(columns(gain, k), (steps, width)) for k in range(pack)], axis=0
+    )
     same = jnp.where(
         (iota2((16, 16), 0) & (steps - 1)) == (iota2((16, 16), 1) & (steps - 1)), 1.0, 0.0
     )
@@ -272,7 +319,7 @@
         same, residual * residual, precision=lax.Precision.HIGHEST, preferred_element_type=f32
     )
     mean_square = jnp.sum(squares, axis=1, keepdims=True) / (pack * width)
-    normed = residual * lax.rsqrt(mean_square + norm_eps) * gain_ref[...].astype(f32)
+    normed = residual * lax.rsqrt(mean_square + norm_eps) * gain
     n_all[my_ep, my_tp] = normed.astype(bf16)
 
     def c_copy(slot, t):
@@ -306,13 +353,13 @@
             into[:, k * width : (k + 1) * width] = flat[k * m : (k + 1) * m]
 
     unpack(n_all[my_ep].reshape(tp * 16, width), tp, x_own)
+    loads[4].wait()
     loads[5].wait()
-    loads[6].wait()
     xo = x_own[...]
     shared_act = (jax.nn.silu(mm(xo, sin_v[0])) * mm(xo, sin_v[1])).astype(bf16)
     sh_v[...] = mm(shared_act, sout_v[...])
+    loads[6].wait()
     loads[7].wait()
-    loads[8].wait()
     for o in range(1, ep):
         chosen_copy(ep_peer(o), ep_peer(o)).wait_recv()
     for p in range(tp):
@@ -343,12 +390,13 @@
         u_ss,
         u_rs,
     )
-    out_ref[...] = (residual + expert_sum).astype(bf16)
+    result = residual + expert_sum
+    for k in range(pack):
+        out_ref[:, k * width : (k + 1) * width] = result[k * steps : (k + 1) * steps].astype(bf16)
 
     @pl.loop(1, n)
     def _(o):
-        d = lax.rem(me + o, n)
-        latent_copy(me, d).wait_send()
+        latent_copy(o).wait_send()
 
     for o in range(1, ep):
         e = ep_peer(o)
@@ -396,25 +444,14 @@
     experts = router.shape[1]
     assert experts == ep
     rp = -(-steps * heads // 16) * 16
-    q = queries[0].reshape(steps, n, heads, kvw).transpose(1, 0, 2, 3).reshape(n, steps * heads, kvw)
-    q = jnp.pad(q, ((0, 0), (0, rp - steps * heads), (0, 0)))
-    new = jnp.pad(new_kv[0], ((0, -steps % 16), (0, 0)))
-    hid = hidden_in[0].reshape(steps, pack, width).transpose(1, 0, 2).reshape(16, width)
-    gain = jnp.repeat(norm_gain.reshape(pack, width), steps, axis=0)
-    e_pad = -(-experts // 16) * 16
-    router_t = jnp.pad(router.T, ((0, e_pad - experts), (0, 0)))
-    picked = expert_ids.reshape(ep_items, expert_ids.shape[2])
-    lanes = lax.broadcasted_iota(jnp.int32, (1, 1, 128), 2)
-    chosen = jnp.sum((picked[:, :, None] == lanes).astype(f32), axis=1)
     q_chunk = min(256, n * rp)
     hf = expert_in.shape[3]
     sf = shared_in.shape[2]
 
     vm, dma = pltpu.VMEM, pltpu.SemaphoreType.DMA
     scratch = [
-        vm((n, rp, kvw), bf16),
-        vm((ctx, kvw), bf16),
-        vm(new.shape, bf16),
+        vm((steps, kvw, n * heads), bf16),
+        vm((kvw, ctx), bf16),
         vm(value_up.shape, bf16),
         vm((heads * vh, d), bf16),
         vm((2, d, hf), bf16),
@@ -437,7 +474,7 @@
         vm((tp, 16, width), bf16),
         vm((tp, 16, width), bf16),
         vm((ep, ep_items, 128), f32),
-        dma((9,)),
+        dma((8,)),
         dma((ep,)),
         dma((ep,)),
         dma((n,)),
@@ -457,10 +494,11 @@
     ]
     vmem = pl.BlockSpec(memory_space=pltpu.VMEM)
     hbm = pl.BlockSpec(memory_space=pl.ANY)
+    smem = pl.BlockSpec(memory_space=pltpu.SMEM)
     out = pl.pallas_call(
         functools.partial(layer_kernel, ep, tp, steps, heads, rp, lat, q_chunk),
-        out_shape=jax.ShapeDtypeStruct((16, width), bf16),
-        in_specs=[pl.BlockSpec(memory_space=pltpu.SMEM)] + [vmem] * 4 + [hbm] * 9,
+        out_shape=jax.ShapeDtypeStruct((steps, d), bf16),
+        in_specs=[smem, vmem, vmem, smem, vmem, vmem] + [hbm] * 8,
         out_specs=vmem,
         scratch_shapes=scratch,
         compiler_params=pltpu.CompilerParams(
@@ -469,13 +507,13 @@
         name="layer",
     )(
         lengths,
-        hid,
-        gain,
-        chosen,
-        router_t,
-        q,
-        kv_cache[0],
-        new,
+        hidden_in[0],
+        norm_gain,
+        expert_ids.transpose(0, 2, 1),
+        router.T,
+        new_kv[0],
+        queries[0].transpose(0, 2, 1),
+        kv_cache[0].T,
         value_up,
         out_proj.reshape(heads * vh, d),
         expert_in[0],
@@ -483,7 +521,7 @@
         shared_in,
         shared_out,
     )
-    return out.reshape(pack, steps, width).transpose(1, 0, 2).reshape(1, steps, d)
+    return out[None]
 
 
 def solution(mesh):

time: 73.6 us -> 60 us (0.82)
  local copies, waits for them, and re-layouts: 12.4 us -> 1.37 us
  Pallas kernels: 59.2 us -> 57.7 us
    reshape x5 -> x0, local copies, waits for them, and re-layouts: 4.97 us -> none  [the longest x1 1.37 us: on_device(): out.reshape(pack, steps, width).transpose(1, 0, 2).reshape(1, steps, d)]
    unnamed x5 -> x1, local copies, waits for them, and re-layouts: 4.62 us -> 1.37 us
    pad x2 -> x0, local copies, waits for them, and re-layouts: 2.7 us -> none  [the longest x1 1.4 us: on_device(): router_t = jnp.pad(router.T, ((0, e_pad - experts), (0, 0)))]
    pallas_call x1, Pallas kernels: 59.2 us -> 57.7 us  [on_device(): pl.pallas_call(functools.partial(layer_kernel, ep, tp, steps, heads, rp,...]
where the time goes in v2:
time: 60 us; the launch traced here: 59.8 us
  Pallas kernels  57.7 us (96%)
  local copies, waits for them, and re-layouts  1.37 us (2%)
  between operations  0.66 us (1%)
    pallas_call x1, Pallas kernels, on_device(): pl.pallas_call(functools.partial(layer_kernel, ep, tp, steps, heads, rp,...  57.7 us
    unnamed x1, local copies, waits for them, and re-layouts  1.37 us

profile of v2, /device:TPU:0, one launch (start us, length us, event | category | flops | bytes accessed | tf_op | source)
XLA Modules:
  0.0 59.8 jit_solution(3868730645644065424)
XLA Ops:
  0.7 57.7 %layer.1 = bf16[4,3584]{1,0:T(4,128)(2,1)} custom-call(s32[1]{0:T(128)S(6)} %copy.16.len_ref, bf16[4,3584]{1,0:T(4,128)(2,1)} %bitcast.20, bf16[3584]{0:T(1024)(128)(2,1)} %gain_ref.1, s32[4,2,4]{2,1,0:T(2,128)} %bitcast.23, bf16[4,3584]{1,0:T(4,128)(2,1)} %bitcast.21, bf16[4,576]{1,0:T(4,128)(2,1)} %bitcast.22, bf16[4,576,128]{2,1,0:T(8,128)(2,1)} %bitcast.18, ...), custom_call_target="tpu_custom_call" | custom-call | tf_op jit(solution)/shard_map/layer/pallas_call | solution.py:498
  58.4 1.4 %copy.17 = bf16[1,4,3584]{2,1,0:T(4,128)(2,1)} copy(bf16[1,4,3584]{2,1,0:T(4,128)(2,1)} %bitcast.19) | data formatting | bytes 57344

commit v3 on v2

--- a/solution.py
+++ b/solution.py
@@ -69,6 +69,8 @@
     lat_send,
     lat_recv,
     vals_v,
+    b_split,
+    b_pair,
     b_send,
     b_recv,
     t_send,
@@ -77,6 +79,8 @@
     x_v,
     x_own,
     sh_v,
+    f_split,
+    f_pair,
     f_send,
     f_recv,
     u_send,
@@ -87,6 +91,8 @@
     ch_rs,
     a_ss,
     a_rs,
+    b_pss,
+    b_prs,
     b_ss,
     b_rs,
     t_ss,
@@ -95,6 +101,10 @@
     c_rs,
     d_ss,
     d_rs,
+    g_ss,
+    g_rs,
+    f_pss,
+    f_prs,
     f_ss,
     f_rs,
     u_ss,
@@ -255,22 +265,45 @@
             by_head[h * items : (h + 1) * items], up_v[h]
         ).astype(bf16)
 
-    def rs_copy(send, recv, ss, rs, k, slot, e):
-        return remote(send.at[k, e], recv.at[k, slot], ss.at[k, e], rs.at[k, slot], {"ep": e})
+    chips = ep // 2
+    my_chip, my_core = my_ep // 2, lax.rem(my_ep, 2)
+    other = {"ep": my_chip * 2 + 1 - my_core}
+
+    def chip_peer(o):
+        return lax.rem(my_chip + o, chips)
+
+    def core_copy(send, pair, ss, rs, k):
+        return remote(send.at[k, 1 - my_core], pair.at[k], ss.at[k], rs.at[k], other)
+
+    def rs_copy(send, recv, ss, rs, k, slot, c):
+        return remote(
+            send.at[k, c], recv.at[k, slot], ss.at[k, c], rs.at[k, slot], {"ep": c * 2 + my_core}
+        )
 
     def tp_copy(send, recv, ss, rs, slot, t):
         return remote(send.at[t], recv.at[slot], ss.at[t], rs.at[slot], {"tp": t})
 
-    def scatter_sum(part, extra, send, recv, ss, rs, send2, recv2, ss2, rs2):
-        for k in range(pack):
-            send[k] = part(k).astype(bf16).reshape(ep, ep_items, width)
-            for o in range(1, ep):
-                rs_copy(send, recv, ss, rs, k, my_ep, ep_peer(o)).start()
-            recv[k, my_ep] = send[k, my_ep]
+    def scatter_sum(part, extra, pairs, chips_bufs, pair_sems, chip_sems, send2, recv2, ss2, rs2):
+        split, pair = pairs
+        send, recv = chips_bufs
+        for k in range(pack + 1):
+            if k < pack:
+                block = part(k).astype(bf16).reshape(chips, 2, ep_items, width)
+                split[k, 0] = block[:, 0]
+                split[k, 1] = block[:, 1]
+                core_copy(split, pair, *pair_sems, k).start()
+            if k > 0:
+                j = k - 1
+                core_copy(split, pair, *pair_sems, j).wait_recv()
+                send[j] = (split[j, my_core].astype(f32) + pair[j].astype(f32)).astype(bf16)
+                for o in range(1, chips):
+                    rs_copy(send, recv, *chip_sems, j, my_chip, chip_peer(o)).start()
+                recv[j, my_chip] = send[j, my_chip]
         sums = []
         for k in range(pack):
-            for o in range(1, ep):
-                rs_copy(send, recv, ss, rs, k, ep_peer(o), ep_peer(o)).wait_recv()
+            for o in range(1, chips):
+                c = chip_peer(o)
+                rs_copy(send, recv, *chip_sems, k, c, c).wait_recv()
             total = jnp.sum(recv[k].astype(f32), axis=0)
             if extra is not None:
                 total = total + extra(k)
@@ -293,10 +326,10 @@
     attention = scatter_sum(
         lambda k: mm(vals, op_v[:, k * width : (k + 1) * width]),
         None,
-        b_send,
-        b_recv,
-        b_ss,
-        b_rs,
+        (b_split, b_pair),
+        (b_send, b_recv),
+        (b_pss, b_prs),
+        (b_ss, b_rs),
         t_send,
         t_recv,
         t_ss,
@@ -327,19 +360,34 @@
             n_all.at[my_ep, my_tp], n_all.at[my_ep, slot], c_ss.at[t], c_rs.at[slot], {"tp": t}
         )
 
-    def d_copy(t, slot, e):
+    def d_copy(t, slot, c):
         return remote(
-            n_all.at[my_ep, t], n_all.at[slot, t], d_ss.at[t, e], d_rs.at[t, slot], {"ep": e}
-        )
+            n_all.at[my_ep, t],
+            n_all.at[slot * 2 + my_core, t],
+            d_ss.at[t, c],
+            d_rs.at[t, slot],
+            {"ep": c * 2 + my_core},
+        )
+
+    def g_copy(t, c):
+        block = n_all.at[c * 2 + my_core, t]
+        return remote(block, block, g_ss.at[t, c], g_rs.at[t, c], other)
+
+    def g_arrival(t, c):
+        block = n_all.at[c * 2 + 1 - my_core, t]
+        return remote(block, block, g_ss.at[t, c], g_rs.at[t, c], other)
+
+    def pass_on(t):
+        for o in range(1, chips):
+            d_copy(t, my_chip, chip_peer(o)).start()
+        g_copy(t, my_chip).start()
 
     for o in range(1, tp):
         c_copy(my_tp, tp_peer(o)).start()
-    for o in range(1, ep):
-        d_copy(my_tp, my_ep, ep_peer(o)).start()
+    pass_on(my_tp)
     for p in range(1, tp):
         c_copy(tp_peer(p), tp_peer(p)).wait_recv()
-        for o in range(1, ep):
-            d_copy(tp_peer(p), my_ep, ep_peer(o)).start()
+        pass_on(tp_peer(p))
 
     def unpack(blocks, count, into):
         m = count * steps
@@ -363,8 +411,12 @@
     for o in range(1, ep):
         chosen_copy(ep_peer(o), ep_peer(o)).wait_recv()
     for p in range(tp):
-        for o in range(1, ep):
-            d_copy(tp_peer(p), ep_peer(o), ep_peer(o)).wait_recv()
+        for o in range(1, chips):
+            d_copy(tp_peer(p), chip_peer(o), chip_peer(o)).wait_recv()
+            g_copy(tp_peer(p), chip_peer(o)).start()
+    for p in range(tp):
+        for o in range(chips):
+            g_arrival(tp_peer(p), chip_peer(o)).wait_recv()
 
     unpack(n_all[...].reshape(n * 16, width), n, x_v)
     x = x_v[...]
@@ -381,10 +433,10 @@
     expert_sum = scatter_sum(
         lambda k: mm(act, eout_v[:, k * width : (k + 1) * width]) * gate,
         lambda k: sh_v[:, k * width : (k + 1) * width],
-        f_send,
-        f_recv,
-        f_ss,
-        f_rs,
+        (f_split, f_pair),
+        (f_send, f_recv),
+        (f_pss, f_prs),
+        (f_ss, f_rs),
         u_send,
         u_recv,
         u_ss,
@@ -401,11 +453,19 @@
     for o in range(1, ep):
         e = ep_peer(o)
         chosen_copy(my_ep, e).wait_send()
+    for k in range(pack):
+        core_copy(b_split, b_pair, b_pss, b_prs, k).wait_send()
+        core_copy(f_split, f_pair, f_pss, f_prs, k).wait_send()
+    for o in range(1, chips):
+        c = chip_peer(o)
         for k in range(pack):
-            rs_copy(b_send, b_recv, b_ss, b_rs, k, my_ep, e).wait_send()
-            rs_copy(f_send, f_recv, f_ss, f_rs, k, my_ep, e).wait_send()
+            rs_copy(b_send, b_recv, b_ss, b_rs, k, my_chip, c).wait_send()
+            rs_copy(f_send, f_recv, f_ss, f_rs, k, my_chip, c).wait_send()
         for p in range(tp):
-            d_copy(tp_peer(p), my_ep, e).wait_send()
+            d_copy(tp_peer(p), my_chip, c).wait_send()
+    for p in range(tp):
+        for o in range(chips):
+            g_copy(tp_peer(p), chip_peer(o)).wait_send()
     for o in range(1, tp):
         t = tp_peer(o)
         tp_copy(t_send, t_recv, t_ss, t_rs, my_tp, t).wait_send()
@@ -436,7 +496,7 @@
     heads, lat, vh = value_up.shape
     kvw = queries.shape[3]
     ctx = kv_cache.shape[1]
-    assert rows == 1 and 16 % steps == 0
+    assert rows == 1 and 16 % steps == 0 and ep % 2 == 0
     pack = 16 // steps
     width = d // pack
     ep_items = tp * steps
@@ -461,16 +521,20 @@
         vm((n, rp, lat), bf16),
         vm((n, rp, lat), bf16),
         vm((items, heads * vh), bf16),
-        vm((pack, ep, ep_items, width), bf16),
-        vm((pack, ep, ep_items, width), bf16),
+        vm((pack, 2, ep // 2, ep_items, width), bf16),
+        vm((pack, ep // 2, ep_items, width), bf16),
+        vm((pack, ep // 2, ep_items, width), bf16),
+        vm((pack, ep // 2, ep_items, width), bf16),
         vm((tp, 16, width), bf16),
         vm((tp, 16, width), bf16),
         vm((ep, tp, 16, width), bf16),
         vm((items, d), bf16),
         vm((ep_items, d), bf16),
         vm((ep_items, d), f32),
-        vm((pack, ep, ep_items, width), bf16),
-        vm((pack, ep, ep_items, width), bf16),
+        vm((pack, 2, ep // 2, ep_items, width), bf16),
+        vm((pack, ep // 2, ep_items, width), bf16),
+        vm((pack, ep // 2, ep_items, width), bf16),
+        vm((pack, ep // 2, ep_items, width), bf16),
         vm((tp, 16, width), bf16),
         vm((tp, 16, width), bf16),
         vm((ep, ep_items, 128), f32),
@@ -479,16 +543,22 @@
         dma((ep,)),
         dma((n,)),
         dma((n,)),
-        dma((pack, ep)),
-        dma((pack, ep)),
+        dma((pack,)),
+        dma((pack,)),
+        dma((pack, ep // 2)),
+        dma((pack, ep // 2)),
         dma((tp,)),
         dma((tp,)),
         dma((tp,)),
         dma((tp,)),
-        dma((tp, ep)),
-        dma((tp, ep)),
-        dma((pack, ep)),
-        dma((pack, ep)),
+        dma((tp, ep // 2)),
+        dma((tp, ep // 2)),
+        dma((tp, ep // 2)),
+        dma((tp, ep // 2)),
+        dma((pack,)),
+        dma((pack,)),
+        dma((pack, ep // 2)),
+        dma((pack, ep // 2)),
         dma((tp,)),
         dma((tp,)),
     ]

time: 60 us -> 57.6 us (0.960)
  Pallas kernels: 57.7 us -> 55.4 us
    pallas_call x1, Pallas kernels: 57.7 us -> 55.4 us  [on_device(): pl.pallas_call(functools.partial(layer_kernel, ep, tp, steps, heads, rp,...]
where the time goes in v3:
time: 57.6 us; the launch traced here: 57.4 us
  Pallas kernels  55.4 us (96%)
  local copies, waits for them, and re-layouts  1.37 us (2%)
  between operations  0.66 us (1%)
    pallas_call x1, Pallas kernels, on_device(): pl.pallas_call(functools.partial(layer_kernel, ep, tp, steps, heads, rp,...  55.4 us
    unnamed x1, local copies, waits for them, and re-layouts  1.37 us

profile of v3, /device:TPU:0, one launch (start us, length us, event | category | flops | bytes accessed | tf_op | source)
XLA Modules:
  0.0 57.4 jit_solution(4759042549100744929)
XLA Ops:
  0.7 55.4 %layer.1 = bf16[4,3584]{1,0:T(4,128)(2,1)} custom-call(s32[1]{0:T(128)S(6)} %copy.16.len_ref, bf16[4,3584]{1,0:T(4,128)(2,1)} %bitcast.20, bf16[3584]{0:T(1024)(128)(2,1)} %gain_ref.1, s32[4,2,4]{2,1,0:T(2,128)} %bitcast.23, bf16[4,3584]{1,0:T(4,128)(2,1)} %bitcast.21, bf16[4,576]{1,0:T(4,128)(2,1)} %bitcast.22, bf16[4,576,128]{2,1,0:T(8,128)(2,1)} %bitcast.18, ...), custom_call_target="tpu_custom_call" | custom-call | tf_op jit(solution)/shard_map/layer/pallas_call | solution.py:568
  56.0 1.4 %copy.17 = bf16[1,4,3584]{2,1,0:T(4,128)(2,1)} copy(bf16[1,4,3584]{2,1,0:T(4,128)(2,1)} %bitcast.19) | data formatting | bytes 57344

commit v4 on v3

--- a/solution.py
+++ b/solution.py
@@ -133,7 +133,7 @@
             ]
         )
     ]
-    for load in loads:
+    for load in loads[:2]:
         load.start()
 
     def dev(d):
@@ -188,6 +188,8 @@
 
     for load in loads[:2]:
         load.wait()
+    for load in loads[2:]:
+        load.start()
     length = len_ref[0]
     dests = q_chunk // rp
     chunks = n // dests

time: 57.6 us -> 57.7 us (level)
  no operation moved by 1% of the time
where the time goes in v4:
time: 57.7 us; the launch traced here: 57.4 us
  Pallas kernels  55.4 us (96%)
  local copies, waits for them, and re-layouts  1.37 us (2%)
  between operations  0.66 us (1%)
    pallas_call x1, Pallas kernels, on_device(): pl.pallas_call(functools.partial(layer_kernel, ep, tp, steps, heads, rp,...  55.4 us
    unnamed x1, local copies, waits for them, and re-layouts  1.37 us

profile of v4, /device:TPU:0, one launch (start us, length us, event | category | flops | bytes accessed | tf_op | source)
XLA Modules:
  0.0 57.4 jit_solution(16840516766259648168)
XLA Ops:
  0.7 55.4 %layer.1 = bf16[4,3584]{1,0:T(4,128)(2,1)} custom-call(s32[1]{0:T(128)S(6)} %copy.16.len_ref, bf16[4,3584]{1,0:T(4,128)(2,1)} %bitcast.20, bf16[3584]{0:T(1024)(128)(2,1)} %gain_ref.1, s32[4,2,4]{2,1,0:T(2,128)} %bitcast.23, bf16[4,3584]{1,0:T(4,128)(2,1)} %bitcast.21, bf16[4,576]{1,0:T(4,128)(2,1)} %bitcast.22, bf16[4,576,128]{2,1,0:T(8,128)(2,1)} %bitcast.18, ...), custom_call_target="tpu_custom_call" | custom-call | tf_op jit(solution)/shard_map/layer/pallas_call | solution.py:570
  56.0 1.4 %copy.17 = bf16[1,4,3584]{2,1,0:T(4,128)(2,1)} copy(bf16[1,4,3584]{2,1,0:T(4,128)(2,1)} %bitcast.19) | data formatting | bytes 57344
